TPU v7x, 512 devices: a whole 4x4x16 slice. The times are simulated.
512 devices in a mesh: clip: 4 (over x), vseq: 32 (over y, z_lo), aseq: 4 (over z_hi, core).
Axes of the slice: x: 4, y: 4, z: 16 (z_hi: 2, z_lo: 8; z = z_hi * 8 + z_lo), core: 2. Of those that a mesh axis runs over, the one named last changes fastest.
Arguments:
- video_q: bfloat16 [98304, 1536], P(('clip', 'vseq'), 'aseq'), parts along dimension 0, may hold values from -9 to 9
- video_k: bfloat16 [98304, 1536], P(('clip', 'vseq'), 'aseq'), parts along dimension 0, may hold values from -9 to 9
- video_v: bfloat16 [98304, 1536], P(('clip', 'vseq'), 'aseq'), parts along dimension 0, may hold values from -6 to 6
- audio_q: bfloat16 [2048, 1536], P(('clip', 'vseq'), 'aseq'), parts along dimension 0, may hold values from -9 to 9
- audio_k: bfloat16 [2048, 1536], P(('clip', 'vseq'), 'aseq'), parts along dimension 0, may hold values from -9 to 9
- audio_v: bfloat16 [2048, 1536], P(('clip', 'vseq'), 'aseq'), parts along dimension 0, may hold values from -6 to 6
- video_cot: bfloat16 [98304, 1536], P(('clip', 'vseq'), 'aseq'), parts along dimension 0, may hold values from -6 to 6
- audio_cot: bfloat16 [2048, 1536], P(('clip', 'vseq'), 'aseq'), parts along dimension 0, may hold values from -6 to 6
Outputs:
- video_out: bfloat16 [98304, 1536], P(('clip', 'vseq'), 'aseq'), parts along dimension 0
- audio_out: bfloat16 [2048, 1536], P(('clip', 'vseq'), 'aseq'), parts along dimension 0
- video_q_grad: bfloat16 [98304, 1536], P(('clip', 'vseq'), 'aseq'), parts along dimension 0
- video_k_grad: bfloat16 [98304, 1536], P(('clip', 'vseq'), 'aseq'), parts along dimension 0
- video_v_grad: bfloat16 [98304, 1536], P(('clip', 'vseq'), 'aseq'), parts along dimension 0
- audio_q_grad: bfloat16 [2048, 1536], P(('clip', 'vseq'), 'aseq'), parts along dimension 0
- audio_k_grad: bfloat16 [2048, 1536], P(('clip', 'vseq'), 'aseq'), parts along dimension 0
- audio_v_grad: bfloat16 [2048, 1536], P(('clip', 'vseq'), 'aseq'), parts along dimension 0
There are 4 independent parts, one for each index of `clip`. A program takes and returns all parts, laid end to end along the dimension named above; each array names one. Nothing has to cross between parts.
All inputs are finite; a program needn't handle non-finite values.
Results may differ from a plain program's by a relative error of at most 0.02005.
Values may be sent and summed in bfloat16 or wider, within the bound.
No kernel may reach another device: no remote copies, remote signals or barrier semaphores. Data moves between devices by JAX's collectives and lax.ppermute only.
A program may use at most 64 MiB of HBM per device.

v0:
```python
import math

import jax
import jax.numpy as jnp
from jax import lax
from jax.sharding import PartitionSpec as P

HDIM = 128


def joined(array, axis, combine):
    everything = jax.tree.map(lambda part: lax.all_gather(part, axis), array)
    first = jax.tree.map(lambda part: part[0], everything)

    def hop(k, so_far):
        return combine(so_far, jax.tree.map(lambda part: part[k], everything))

    return lax.fori_loop(1, lax.axis_size(axis), hop, first)


def by_heads(matrix):
    return matrix.reshape(matrix.shape[0], -1, HDIM)


def softmax_pair(earlier, later):
    larger = jnp.maximum(earlier[0], later[0])
    return (
        larger,
        earlier[1] * jnp.exp(earlier[0] - larger) + later[1] * jnp.exp(later[0] - larger),
    )


def body(video_q, video_k, video_v, audio_q, audio_k, audio_v, video_cot, audio_cot):
    factor = 1.0 / math.sqrt(HDIM)
    video_rows = video_q.shape[0]
    local_audio = audio_q.shape[0]
    col_count = video_q.shape[1]
    keys_all, values_all, queries_all, cot_all = (
        lax.all_gather(audio_k, "vseq", axis=0, tiled=True),
        lax.all_gather(audio_v, "vseq", axis=0, tiled=True),
        lax.all_gather(audio_q, "vseq", axis=0, tiled=True),
        lax.all_gather(audio_cot, "vseq", axis=0, tiled=True),
    )
    vid_query = by_heads(video_q)
    vid_key = by_heads(video_k)
    vid_value = by_heads(video_v)
    vid_cot = by_heads(video_cot)
    aud_key = by_heads(keys_all)
    aud_value = by_heads(values_all)
    aud_query = by_heads(queries_all)
    aud_cot = by_heads(cot_all)
    scores = (
        jnp.einsum("vhd,ahd->hva", vid_query, aud_key, preferred_element_type=jnp.float32) * factor
    )
    row_peak = jnp.max(scores, axis=2, keepdims=True)
    logsum = row_peak + jnp.log(jnp.sum(jnp.exp(scores - row_peak), axis=2, keepdims=True))
    weights = jnp.exp(scores - logsum).astype(jnp.bfloat16)
    video_out = jnp.einsum(
        "hva,ahd->vhd", weights, aud_value, preferred_element_type=jnp.float32
    ).astype(jnp.bfloat16)
    row_delta = jnp.sum(vid_cot.astype(jnp.float32) * video_out.astype(jnp.float32), axis=2)
    dweights = jnp.einsum("vhd,ahd->hva", vid_cot, aud_value, preferred_element_type=jnp.float32)
    grad_scores = (
        weights.astype(jnp.float32) * (dweights - row_delta.T[:, :, None]) * factor
    ).astype(jnp.bfloat16)
    video_q_grad = jnp.einsum(
        "hva,ahd->vhd", grad_scores, aud_key, preferred_element_type=jnp.float32
    ).astype(jnp.bfloat16)
    cross_scores = (
        jnp.einsum("ahd,vhd->hav", aud_query, vid_key, preferred_element_type=jnp.float32) * factor
    )
    local_peak = jnp.max(cross_scores, axis=2)
    local_total = jnp.sum(jnp.exp(cross_scores - local_peak[:, :, None]), axis=2)
    first_row = lax.axis_index("vseq") * local_audio
    best_peak, sum_total = joined((local_peak, local_total), "vseq", softmax_pair)
    cross_logsum = best_peak + jnp.log(sum_total)
    cross_weights = jnp.exp(cross_scores - cross_logsum[:, :, None]).astype(jnp.bfloat16)
    partial_out = jnp.einsum(
        "hav,vhd->ahd", cross_weights, vid_value, preferred_element_type=jnp.float32
    ).reshape(-1, col_count)
    summed_out = lax.psum(partial_out, "vseq").astype(jnp.bfloat16)
    audio_out = lax.dynamic_slice_in_dim(summed_out, first_row, local_audio, 0)
    cross_delta = jnp.sum(
        aud_cot.astype(jnp.float32) * by_heads(summed_out).astype(jnp.float32), axis=2
    )
    cross_dweights = jnp.einsum(
        "ahd,vhd->hav", aud_cot, vid_value, preferred_element_type=jnp.float32
    )
    cross_grads = (
        cross_weights.astype(jnp.float32) * (cross_dweights - cross_delta.T[:, :, None]) * factor
    ).astype(jnp.bfloat16)
    video_k_grad = jnp.einsum(
        "hav,ahd->vhd", cross_grads, aud_query, preferred_element_type=jnp.float32
    ).astype(jnp.bfloat16)
    video_v_grad = jnp.einsum(
        "hav,ahd->vhd", cross_weights, aud_cot, preferred_element_type=jnp.float32
    ).astype(jnp.bfloat16)
    key_term = jnp.einsum(
        "hva,vhd->ahd", grad_scores, vid_query, preferred_element_type=jnp.float32
    )
    value_term = jnp.einsum("hva,vhd->ahd", weights, vid_cot, preferred_element_type=jnp.float32)
    pair_sums = lax.psum_scatter(
        jnp.concatenate(
            [
                key_term.reshape(local_audio * lax.axis_size("vseq"), col_count),
                value_term.reshape(local_audio * lax.axis_size("vseq"), col_count),
            ],
            axis=1,
        ),
        "vseq",
        scatter_dimension=0,
        tiled=True,
    )
    query_term = jnp.einsum(
        "hav,vhd->ahd", cross_grads, vid_key, preferred_element_type=jnp.float32
    )
    query_sums = lax.psum_scatter(
        query_term.reshape(local_audio * lax.axis_size("vseq"), col_count),
        "vseq",
        scatter_dimension=0,
        tiled=True,
    )
    summed = jnp.concatenate([pair_sums, query_sums], axis=1)
    audio_k_grad = summed[:, :col_count].astype(jnp.bfloat16)
    audio_v_grad = summed[:, col_count : 2 * col_count].astype(jnp.bfloat16)
    audio_q_grad = summed[:, 2 * col_count :].astype(jnp.bfloat16)
    return (
        video_out.reshape(video_rows, col_count),
        audio_out,
        video_q_grad.reshape(video_rows, col_count),
        video_k_grad.reshape(video_rows, col_count),
        video_v_grad.reshape(video_rows, col_count),
        audio_q_grad,
        audio_k_grad,
        audio_v_grad,
    )


def solution(mesh):
    placed = (
        P(("clip", "vseq"), "aseq"),
        P(("clip", "vseq"), "aseq"),
        P(("clip", "vseq"), "aseq"),
        P(("clip", "vseq"), "aseq"),
        P(("clip", "vseq"), "aseq"),
        P(("clip", "vseq"), "aseq"),
        P(("clip", "vseq"), "aseq"),
        P(("clip", "vseq"), "aseq"),
    )
    return jax.shard_map(
        body,
        mesh=mesh,
        in_specs=placed,
        out_specs=(
            P(("clip", "vseq"), "aseq"),
            P(("clip", "vseq"), "aseq"),
            P(("clip", "vseq"), "aseq"),
            P(("clip", "vseq"), "aseq"),
            P(("clip", "vseq"), "aseq"),
            P(("clip", "vseq"), "aseq"),
            P(("clip", "vseq"), "aseq"),
            P(("clip", "vseq"), "aseq"),
        ),
        check_vma=False,
    )
```

profile of v0, /device:TPU:2, one launch (start us, length us, event | category | flops | bytes accessed | tf_op | source)
XLA Modules:
  0.0 1249.4 jit_solution(10445010328548963062)
XLA Ops:
  7.2 129.1 %all_gather.26 = bf16[512,384]{1,0:T(8,128)(2,1)S(1)} all-gather(bf16[16,384]{1,0:T(8,128)(2,1)} %param.13), channel_id=1, replica_groups=mesh['clip'=4,'vseq'=32,'aseq'=4] {'vseq'}, dimensions={0}, use_global_device_ids=true | all-gather | bytes 405504 | tf_op jit(solution)/shard_map/all_gather | solution.py:41
  136.5 114.7 %all_gather.31 = bf16[512,384]{1,0:T(8,128)(2,1)S(1)} all-gather(bf16[16,384]{1,0:T(8,128)(2,1)} %param.17), channel_id=1, replica_groups=mesh['clip'=4,'vseq'=32,'aseq'=4] {'vseq'}, dimensions={0}, use_global_device_ids=true | all-gather | bytes 405504 | tf_op jit(solution)/shard_map/all_gather | solution.py:42
  252.8 2.1 copy.81
  255.8 2.1 copy-done
  259.0 115.6 %all-gather.3 = f32[32,3,512]{2,1,0:T(4,128)S(1)} all-gather(f32[1,3,512]{2,1,0:T(4,128)S(1)} %bitcast.111), channel_id=3, replica_groups=mesh['clip'=4,'vseq'=32,'aseq'=4] {'vseq'}, dimensions={0}, use_global_device_ids=true | all-gather | bytes 202752 | tf_op jit(solution)/shard_map/all_gather | solution.py:12
  374.6 113.8 %all-gather.2 = f32[32,3,512]{2,1,0:T(4,128)S(1)} all-gather(f32[1,3,512]{2,1,0:T(4,128)S(1)} %bitcast.108), channel_id=2, replica_groups=mesh['clip'=4,'vseq'=32,'aseq'=4] {'vseq'}, dimensions={0}, use_global_device_ids=true | all-gather | bytes 202752 | tf_op jit(solution)/shard_map/all_gather | solution.py:12
  490.0 3.1 exponential_convert_fusion
  493.1 2.8 fusion.4
  495.9 239.8 %all-reduce.1 = bf16[512,384]{0,1:T(8,128)(2,1)} all-reduce(f32[512,384]{0,1:T(8,128)} %bitcast.101), channel_id=1, replica_groups=mesh['clip'=4,'vseq'=32,'aseq'=4] {'vseq'}, use_global_device_ids=true, to_apply=%region_6.0 | all-reduce | flops 196608 | bytes 1179648 | tf_op jit(solution)/shard_map/psum | solution.py:81
  742.1 2.3 copy.90
  744.5 115.4 %all_gather.24 = bf16[512,384]{1,0:T(8,128)(2,1)S(1)} all-gather(bf16[16,384]{1,0:T(8,128)(2,1)S(1)} %copy-done.9), channel_id=1, replica_groups=mesh['clip'=4,'vseq'=32,'aseq'=4] {'vseq'}, dimensions={0}, use_global_device_ids=true | all-gather | bytes 405504 | tf_op jit(solution)/shard_map/all_gather | solution.py:39
  865.1 2.1 exponential_convert_fusion.1
  867.2 116.5 %all_gather.25 = bf16[512,384]{1,0:T(8,128)(2,1)S(1)} all-gather(bf16[16,384]{1,0:T(8,128)(2,1)S(1)} %copy-done.10), channel_id=1, replica_groups=mesh['clip'=4,'vseq'=32,'aseq'=4] {'vseq'}, dimensions={0}, use_global_device_ids=true | all-gather | bytes 405504 | tf_op jit(solution)/shard_map/all_gather | solution.py:40
  986.0 3.4 fusion.7
  989.4 2.3 copy.94
  991.7 3.2 multiply_reduce_fusion.2
  994.9 2.7 multiply_convert_fusion.1
  1001.1 2.7 pad_maximum_fusion
  1005.1 2.3 copy.99
  1009.1 3.0 convolution_convert_fusion.1
  1012.0 2.1 copy.98
  1014.2 2.1 copy.95
  1017.6 2.1 copy.97
  1021.0 220.1 %reduce-scatter.5.cloned.1.call-done = f32[16,768]{1,0:T(8,128)} async-done(((f32[512,768]{1,0:T(8,128)}), f32[16,768]{1,0:T(8,128)}) %reduce-scatter.5.cloned.1.call-update) | async-done | bytes 49168 | tf_op jit(solution)/shard_map/reduce_scatter | solution.py:102
  (85 shorter events, 30.5 us)
Async XLA Ops:
  7.2 1012.5 %reduce-scatter.3.cloned.1.call-start = ((), (), s32[]{:S(2)}) async-start(), calls=%async_computation.2 | async-start | bytes 811008 | tf_op jit(solution)/shard_map/reduce_scatter | solution.py:117
  136.5 122.5 %copy-start.6 = (bf16[512,384]{0,1:T(8,128)(2,1)}, bf16[512,384]{0,1:T(8,128)(2,1)S(1)}, u32[]{:S(2)}) copy-start(bf16[512,384]{0,1:T(8,128)(2,1)S(1)} %copy.77) | copy-start | bytes 1179652
  255.8 2.1 copy-start
  736.8 7.7 copy-start.9
  738.9 1.4 copy-start.1
  744.5 496.7 %reduce-scatter.5.cloned.1.call-start = ((), (), s32[]{:S(2)}) async-start(), calls=%async_computation.3 | async-start | bytes 1622016 | tf_op jit(solution)/shard_map/reduce_scatter | solution.py:102
  862.2 2.8 copy-start.4
  865.1 2.2 copy-start.10
  991.7 7.3 copy-start.5
  997.6 1.4 copy-start.2
  1001.1 8.0 copy-start.7
  1003.8 12.5 copy-start.8
  1005.1 11.2 copy-start.3
Sparse Core Ops, SparseCore 0:
  744.6 235.5 reduce-scatter.2
  1003.9 237.1 reduce-scatter.4
where the time goes:
time: 1250 us
  blocking collectives  945 us (76%)
  waiting for transfers between devices  220 us (18%)
  local copies, waits for them, and re-layouts  29.9 us (2%)
  matrix products  25.4 us (2%)
  between operations  14.2 us (1%)
  other arithmetic  14 us (1%)
    psum x1, blocking collectives, body(): summed_out = lax.psum(partial_out, 'vseq').astype(jnp.bfloat16)  240 us
    all_gather x2, blocking collectives, joined(): everything = jax.tree.map(lambda part: lax.all_gather(part, axis), array)  229 us
    reduce_scatter x1, waiting for transfers between devices, body(): lax.psum_scatter(jnp.concatenate([key_term.reshape(local_audio * lax.axis...  220 us
    all_gather x1, blocking collectives, body(): lax.all_gather(audio_q, 'vseq', axis=0, tiled=True)  129 us
    all_gather x1, blocking collectives, body(): lax.all_gather(audio_v, 'vseq', axis=0, tiled=True)  117 us
    all_gather x1, blocking collectives, body(): lax.all_gather(audio_k, 'vseq', axis=0, tiled=True)  115 us
    all_gather x1, blocking collectives, body(): lax.all_gather(audio_cot, 'vseq', axis=0, tiled=True)  115 us
  transfers between devices with their start and end apart: 2, of which 1 were waited for; matrix products, arithmetic and copies ran while one was open for 3% of the time, Pallas kernels for 0%

commit v1 on v0

v1 whole, which is shorter than its diff:
```python
import functools
import math

import jax
import jax.numpy as jnp
from jax import lax
from jax.experimental import pallas as pl
from jax.experimental.pallas import tpu as pltpu
from jax.sharding import PartitionSpec as P

HDIM = 128
YS, ZS = 4, 8
SCALE = 1.0 / math.sqrt(HDIM)
SCALE2 = SCALE / math.log(2.0)
F32, BF16 = jnp.float32, jnp.bfloat16


def z_swap(d):
    return [(y * ZS + z, y * ZS + (z ^ d)) for y in range(YS) for z in range(ZS)]


def y_shift(j):
    return [(y * ZS + z, ((y + j) % YS) * ZS + z) for y in range(YS) for z in range(ZS)]


def gather_rows(block):
    for d in (4, 2, 1):
        block = jnp.concatenate([block, lax.ppermute(block, "vseq", z_swap(d))], axis=0)
    return [block] + [lax.ppermute(block, "vseq", y_shift(-j)) for j in range(1, YS)]


def scatter_rows(own, others):
    total = own
    for j in range(1, YS):
        total = total + lax.ppermute(others[j - 1], "vseq", y_shift(j)).astype(F32)
    for d in (1, 2, 4):
        half = total.shape[0] // 2
        got = lax.ppermute(total[half:].astype(BF16), "vseq", z_swap(d))
        total = total[:half] + got.astype(F32)
    return total


def nt(a, b):
    return lax.dot_general(a, b, (((1,), (1,)), ((), ())), preferred_element_type=F32)


def nn(a, b):
    return lax.dot_general(a, b, (((1,), (0,)), ((), ())), preferred_element_type=F32)


def joined(refs):
    return jnp.concatenate([ref[...] for ref in refs], axis=0)


def put_pieces(own_ref, other_refs, left, right):
    rows = own_ref.shape[0]
    for j, ref in enumerate([own_ref] + list(other_refs)):
        cut = slice(j * rows, (j + 1) * rows)
        ref[:, :HDIM] = left[:, cut].T.astype(ref.dtype)
        ref[:, HDIM:] = right[:, cut].T.astype(ref.dtype)


def video_kernel(chunk, q_ref, cot_ref, *refs):
    keys, values = joined(refs[0:4]), joined(refs[4:8])
    out_ref, qgrad_ref, own_ref = refs[8:11]
    key_sum = value_sum = None
    for at in range(0, q_ref.shape[0], chunk):
        rows = pl.ds(at, chunk)
        q, cot = q_ref[rows, :], cot_ref[rows, :]
        scores = nt(q, keys)
        peak = jnp.max(scores, axis=1, keepdims=True)
        e = jnp.exp2((scores - peak) * SCALE2)
        p = e * (1.0 / jnp.sum(e, axis=1, keepdims=True))
        pb = p.astype(BF16)
        out = nn(pb, values).astype(BF16)
        out_ref[rows, :] = out
        delta = jnp.sum(cot.astype(F32) * out.astype(F32), axis=1, keepdims=True)
        ds = (p * (nt(cot, values) - delta)).astype(BF16)
        qgrad_ref[rows, :] = (nn(ds, keys) * SCALE).astype(BF16)
        key_part, value_part = nn(q.T, ds), nn(cot.T, pb)
        key_sum = key_part if key_sum is None else key_sum + key_part
        value_sum = value_part if value_sum is None else value_sum + value_part
    put_pieces(own_ref, refs[11:14], key_sum * SCALE, value_sum)


def stats_kernel(chunk, k_ref, v_ref, *refs):
    queries, cots = joined(refs[0:4]), joined(refs[4:8])
    stats_ref, s_ref = refs[8:10]
    peak = None
    for at in range(0, k_ref.shape[0], chunk):
        rows = pl.ds(at, chunk)
        scores = nt(k_ref[rows, :], queries) * SCALE2
        s_ref[rows, :] = scores
        top = jnp.max(scores, axis=0, keepdims=True)
        peak = top if peak is None else jnp.maximum(peak, top)
    total = weighted = jnp.zeros_like(peak)
    for at in range(0, k_ref.shape[0], chunk):
        rows = pl.ds(at, chunk)
        e = jnp.exp2(s_ref[rows, :] - peak)
        total = total + jnp.sum(e, axis=0, keepdims=True)
        weighted = weighted + jnp.sum(e * nt(v_ref[rows, :], cots), axis=0, keepdims=True)
    stats_ref[0, 0:1, :] = peak
    stats_ref[0, 1:2, :] = total
    stats_ref[0, 2:3, :] = weighted
    stats_ref[0, 3:8, :] = jnp.zeros((5, peak.shape[1]), F32)


def swapped(x, d):
    if d == 0:
        return x
    width = x.shape[1] // YS
    size = (width // ZS) * {4: 1, 2: 2, 1: 4}[d]
    parts = [x[:, at : at + size] for at in range(0, x.shape[1], size)]
    return jnp.concatenate([parts[i ^ 1] for i in range(len(parts))], axis=1)


def turned(x, j):
    width = x.shape[1] // YS
    parts = [x[:, i * width : (i + 1) * width] for i in range(YS)]
    return jnp.concatenate([parts[(i + j) % YS] for i in range(YS)], axis=1)


def merge_kernel(d, own_ref, *refs):
    merged_ref = refs[-1]
    for head in range(own_ref.shape[0]):
        terms = [own_ref[head]]
        for j, ref in enumerate(refs[:-1]):
            terms.append(swapped(ref[head], d) if d else turned(ref[head], j + 1))
        peak = functools.reduce(jnp.maximum, [t[0:1] for t in terms])
        merged_ref[head] = jnp.concatenate(
            [peak, sum(t[1:] * jnp.exp2(t[0:1] - peak) for t in terms)], axis=0
        )


def merge(d, own, others):
    return pl.pallas_call(
        functools.partial(merge_kernel, d),
        out_shape=jax.ShapeDtypeStruct(own.shape, F32),
    )(own, *others)


def audio_kernel(chunk, stats_ref, k_ref, v_ref, *refs):
    queries, cots = joined(refs[0:4]), joined(refs[4:8])
    kgrad_ref, vgrad_ref, own_ref = refs[8:11]
    logsum = stats_ref[0, 0:1, :] + jnp.log2(stats_ref[0, 1:2, :])
    delta = stats_ref[0, 2:3, :] / stats_ref[0, 1:2, :]
    out_sum = query_sum = None
    for at in range(0, k_ref.shape[0], chunk):
        rows = pl.ds(at, chunk)
        k, v = k_ref[rows, :], v_ref[rows, :]
        p = jnp.exp2(nt(k, queries) * SCALE2 - logsum)
        pb = p.astype(BF16)
        ds = (p * (nt(v, cots) - delta)).astype(BF16)
        vgrad_ref[rows, :] = nn(pb, cots).astype(BF16)
        kgrad_ref[rows, :] = (nn(ds, queries) * SCALE).astype(BF16)
        out_part, query_part = nn(v.T, pb), nn(k.T, ds)
        out_sum = out_part if out_sum is None else out_sum + out_part
        query_sum = query_part if query_sum is None else query_sum + query_part
    put_pieces(own_ref, refs[11:14], out_sum, query_sum * SCALE)


def specs(video_rows, piece_rows, heads):
    by_head = pl.BlockSpec((video_rows, HDIM), lambda h: (0, h))
    first = [pl.BlockSpec((piece_rows, HDIM), lambda h: (0, h))] * YS
    second = [pl.BlockSpec((piece_rows, HDIM), lambda h: (0, heads + h))] * YS
    sums = [pl.BlockSpec((piece_rows, 2 * HDIM), lambda h: (0, h))] * YS
    return by_head, first + second, sums


def piece_shapes(piece_rows, heads):
    return [
        jax.ShapeDtypeStruct((piece_rows, heads * 2 * HDIM), F32 if j == 0 else BF16)
        for j in range(YS)
    ]


PARAMS = pltpu.CompilerParams(vmem_limit_bytes=40 * 1024 * 1024)


def unpaired(pairs):
    both = pairs.reshape(pairs.shape[0], -1, 2, HDIM)
    return [both[:, :, i].reshape(pairs.shape[0], -1).astype(BF16) for i in range(2)]


def body(video_q, video_k, video_v, audio_q, audio_k, audio_v, video_cot, audio_cot):
    rows, cols = video_q.shape
    heads = cols // HDIM
    chunk = math.gcd(rows, 256)
    audio_rows = audio_q.shape[0] * YS * ZS
    query_pieces = gather_rows(jnp.concatenate([audio_q, audio_cot], axis=1))
    key_pieces = gather_rows(jnp.concatenate([audio_k, audio_v], axis=1))
    by_head, piece_specs, sum_specs = specs(rows, audio_rows // YS, heads)
    stats_spec = pl.BlockSpec((1, 8, audio_rows), lambda h: (h, 0, 0))
    like = jax.ShapeDtypeStruct((rows, cols), BF16)
    pieces = piece_shapes(audio_rows // YS, heads)

    stats = pl.pallas_call(
        functools.partial(stats_kernel, chunk),
        grid=(heads,),
        in_specs=[by_head] * 2 + piece_specs,
        out_specs=stats_spec,
        out_shape=jax.ShapeDtypeStruct((heads, 8, audio_rows), F32),
        scratch_shapes=[pltpu.VMEM((rows, audio_rows), F32)],
        compiler_params=PARAMS,
        name="audio_stats",
    )(video_k, video_v, *query_pieces, *query_pieces)
    stats = merge(0, stats, [lax.ppermute(stats, "vseq", y_shift(j)) for j in range(1, YS)])
    for d in (1, 2, 4):
        stats = merge(d, stats, [lax.ppermute(stats, "vseq", z_swap(d))])

    video_out, video_q_grad, *key_sums = pl.pallas_call(
        functools.partial(video_kernel, chunk),
        grid=(heads,),
        in_specs=[by_head] * 2 + piece_specs,
        out_specs=[by_head] * 2 + sum_specs,
        out_shape=[like] * 2 + pieces,
        compiler_params=PARAMS,
        name="video_queries",
    )(video_q, video_cot, *key_pieces, *key_pieces)
    audio_k_grad, audio_v_grad = unpaired(scatter_rows(key_sums[0], key_sums[1:]))

    video_k_grad, video_v_grad, *query_sums = pl.pallas_call(
        functools.partial(audio_kernel, chunk),
        grid=(heads,),
        in_specs=[stats_spec] + [by_head] * 2 + piece_specs,
        out_specs=[by_head] * 2 + sum_specs,
        out_shape=[like] * 2 + pieces,
        compiler_params=PARAMS,
        name="audio_queries",
    )(stats, video_k, video_v, *query_pieces, *query_pieces)
    audio_out, audio_q_grad = unpaired(scatter_rows(query_sums[0], query_sums[1:]))
    return (
        video_out,
        audio_out,
        video_q_grad,
        video_k_grad,
        video_v_grad,
        audio_q_grad,
        audio_k_grad,
        audio_v_grad,
    )


def solution(mesh):
    placed = (P(("clip", "vseq"), "aseq"),) * 8
    return jax.shard_map(body, mesh=mesh, in_specs=placed, out_specs=placed, check_vma=False)
```

time: 1250 us -> 168 us (0.13)
  the two profiles are of different devices: /device:TPU:2 before, /device:TPU:34 now
where the time goes in v1:
time: 168 us; the launch traced here: 167 us
  starting transfers between devices  104 us (62%)
  waiting for transfers between devices  32.7 us (19%)
  Pallas kernels  22.3 us (13%)
  local copies, waits for them, and re-layouts  5.62 us (3%)
    ppermute x6, starting transfers between devices, gather_rows(): lax.ppermute(block, 'vseq', z_swap(d))  26.8 us
    ppermute x6, starting transfers between devices, gather_rows(): lax.ppermute(block, 'vseq', y_shift(-j))  20.8 us
    ppermute x6, starting transfers between devices, scatter_rows(): got = lax.ppermute(total[half:].astype(BF16), 'vseq', z_swap(d))  20.3 us
    ppermute x6, starting transfers between devices, scatter_rows(): total = total + lax.ppermute(others[j - 1], 'vseq', y_shift(j)).astype(F32)  20.1 us
    ppermute x6, waiting for transfers between devices, scatter_rows(): got = lax.ppermute(total[half:].astype(BF16), 'vseq', z_swap(d))  12.9 us
    pallas_call x1, Pallas kernels, body(): pl.pallas_call(functools.partial(video_kernel, chunk), grid=(heads,), in_...  8.48 us
    ppermute x3, starting transfers between devices, body(): stats = merge(d, stats, [lax.ppermute(stats, 'vseq', z_swap(d))])  8.33 us
    ppermute x3, starting transfers between devices, body(): lax.ppermute(stats, 'vseq', y_shift(j))  7.28 us
  transfers between devices with their start and end apart: 30, of which 13 were waited for; matrix products, arithmetic and copies ran while one was open for 1% of the time, Pallas kernels for 13%

profile of v1, /device:TPU:34, one launch (start us, length us, event | category | flops | bytes accessed | tf_op | source)
XLA Modules:
  0.0 166.9 jit_solution(7365580012730192899)
XLA Ops:
  1.4 9.1 %collective-permute-start = (bf16[16,768]{1,0:T(8,128)(2,1)S(1)}, bf16[16,768]{1,0:T(8,128)(2,1)S(1)}, u32[]{:S(2)}, u32[]{:S(2)}) collective-permute-start(bf16[16,768]{1,0:T(8,128)(2,1)S(1)} %constant_dynamic-update-slice_fusion), channel_id=1, source_target_pairs={{0,16},{4,20},{8,24},{12,28},{16,0},{20,4},{24,8},{28,12},{32,48},... | collective-permute-start | bytes 73736 | tf_op jit(solution)/shard_map/ppermute | solution.py:28
  12.5 5.2 %collective-permute-start.1 = (bf16[32,768]{1,0:T(8,128)(2,1)S(1)}, bf16[32,768]{1,0:T(8,128)(2,1)S(1)}, u32[]{:S(2)}, u32[]{:S(2)}) collective-permute-start(bf16[32,768]{1,0:T(8,128)(2,1)S(1)} %pad_maximum_fusion.4), channel_id=1, source_target_pairs={{0,8},{4,12},{8,0},{12,4},{16,24},{20,28},{24,16},{28,20},{32,40},... | collective-permute-start | bytes 147464 | tf_op jit(solution)/shard_map/ppermute | solution.py:28
  20.4 5.1 %collective-permute-start.7 = (bf16[32,768]{1,0:T(8,128)(2,1)S(1)}, bf16[32,768]{1,0:T(8,128)(2,1)S(1)}, u32[]{:S(2)}, u32[]{:S(2)}) collective-permute-start(bf16[32,768]{1,0:T(8,128)(2,1)S(1)} %pad_maximum_fusion.5), channel_id=1, source_target_pairs={{0,8},{4,12},{8,0},{12,4},{16,24},{20,28},{24,16},{28,20},{32,40},... | collective-permute-start | bytes 147464 | tf_op jit(solution)/shard_map/ppermute | solution.py:28
  28.1 3.3 %collective-permute-start.8 = (bf16[64,768]{1,0:T(8,128)(2,1)S(1)}, bf16[64,768]{1,0:T(8,128)(2,1)S(1)}, u32[]{:S(2)}, u32[]{:S(2)}) collective-permute-start(bf16[64,768]{1,0:T(8,128)(2,1)S(1)} %pad_maximum_fusion.3), channel_id=1, source_target_pairs={{0,4},{4,0},{8,12},{12,8},{16,20},{20,16},{24,28},{28,24},{32,36},... | collective-permute-start | bytes 294920 | tf_op jit(solution)/shard_map/ppermute | solution.py:28
  32.2 3.5 %collective-permute-start.5 = (bf16[128,768]{1,0:T(8,128)(2,1)S(1)}, bf16[128,768]{1,0:T(8,128)(2,1)S(1)}, u32[]{:S(2)}, u32[]{:S(2)}) collective-permute-start(bf16[128,768]{1,0:T(8,128)(2,1)S(1)} %pad_maximum_fusion.refs_0_.refs_4_), channel_id=1, source_target_pairs={{0,32},{4,36},{8,40},{12,44},{16,48},{20,52},{24,56},{28,60},{32,6... | collective-permute-start | bytes 589832 | tf_op jit(solution)/shard_map/ppermute | solution.py:29
  35.7 4.8 %collective-permute-start.4 = (bf16[128,768]{1,0:T(8,128)(2,1)S(1)}, bf16[128,768]{1,0:T(8,128)(2,1)S(1)}, u32[]{:S(2)}, u32[]{:S(2)}) collective-permute-start(bf16[128,768]{1,0:T(8,128)(2,1)S(1)} %pad_maximum_fusion.refs_0_.refs_4_), channel_id=1, source_target_pairs={{0,64},{4,68},{8,72},{12,76},{16,80},{20,84},{24,88},{28,92},{32,9... | collective-permute-start | bytes 589832 | tf_op jit(solution)/shard_map/ppermute | solution.py:29
  40.5 3.3 %collective-permute-start.3 = (bf16[128,768]{1,0:T(8,128)(2,1)S(1)}, bf16[128,768]{1,0:T(8,128)(2,1)S(1)}, u32[]{:S(2)}, u32[]{:S(2)}) collective-permute-start(bf16[128,768]{1,0:T(8,128)(2,1)S(1)} %pad_maximum_fusion.refs_0_.refs_4_), channel_id=1, source_target_pairs={{0,96},{4,100},{8,104},{12,108},{16,112},{20,116},{24,120},{28,124... | collective-permute-start | bytes 589832 | tf_op jit(solution)/shard_map/ppermute | solution.py:29
  49.3 3.8 %collective-permute-start.9 = (bf16[128,768]{1,0:T(8,128)(2,1)S(1)}, bf16[128,768]{1,0:T(8,128)(2,1)S(1)}, u32[]{:S(2)}, u32[]{:S(2)}) collective-permute-start(bf16[128,768]{1,0:T(8,128)(2,1)S(1)} %pad_maximum_fusion.1.refs_0_.refs_4_), channel_id=1, source_target_pairs={{0,96},{4,100},{8,104},{12,108},{16,112},{20,116},{24,120},{28,124... | collective-permute-start | bytes 589832 | tf_op jit(solution)/shard_map/ppermute | solution.py:29
  53.2 8.5 %video_queries.1 = (bf16[768,384]{1,0:T(8,128)(2,1)}, bf16[768,384]{1,0:T(8,128)(2,1)}, f32[128,768]{1,0:T(8,128)S(1)}, bf16[128,768]{1,0:T(8,128)(2,1)S(1)}, bf...) custom-call(bf16[768,384]{1,0:T(8,128)(2,1)S(1)} %copy-done.2, bf16[768,384]{1,0:T(8,128)(2,1)S(1)} %copy-done.3, ...), custom_call_target="tpu_custom_call" | custom-call | tf_op jit(solution)/shard_map/video_queries/pallas_call | solution.py:211
  64.3 4.0 %collective-permute-start.25 = (bf16[128,768]{1,0:T(8,128)(2,1)S(1)}, bf16[128,768]{1,0:T(8,128)(2,1)S(1)}, u32[]{:S(2)}, u32[]{:S(2)}) collective-permute-start(bf16[128,768]{1,0:T(8,128)(2,1)S(1)} %get-tuple-element.30), channel_id=1, source_target_pairs={{0,64},{4,68},{8,72},{12,76},{16,80},{20,84},{24,88},{28,92},{32,9... | collective-permute-start | bytes 589832 | tf_op jit(solution)/shard_map/ppermute | solution.py:35
  68.3 4.5 %collective-permute-start.26 = (bf16[128,768]{1,0:T(8,128)(2,1)S(1)}, bf16[128,768]{1,0:T(8,128)(2,1)}, u32[]{:S(2)}, u32[]{:S(2)}) collective-permute-start(bf16[128,768]{1,0:T(8,128)(2,1)S(1)} %get-tuple-element.31), channel_id=1, source_target_pairs={{0,96},{4,100},{8,104},{12,108},{16,112},{20,116},{24,120},{28,124... | collective-permute-start | bytes 589832 | tf_op jit(solution)/shard_map/ppermute | solution.py:35
  77.5 3.4 %collective-permute-start.13 = (f32[3,8,512]{2,1,0:T(8,128)S(1)}, f32[3,8,512]{2,1,0:T(8,128)S(1)}, u32[]{:S(2)}, u32[]{:S(2)}) collective-permute-start(f32[3,8,512]{2,1,0:T(8,128)S(1)} %audio_stats.1.own_ref), channel_id=1, source_target_pairs={{0,64},{4,68},{8,72},{12,76},{16,80},{20,84},{24,88},{28,92},{32,9... | collective-permute-start | bytes 147464 | tf_op jit(solution)/shard_map/ppermute | solution.py:207
  85.0 3.8 %collective-permute-done.12.refs_0_ = f32[3,8,512]{2,1,0:T(8,128)S(1)} collective-permute-done((f32[3,8,512]{2,1,0:T(8,128)S(1)}, f32[3,8,512]{2,1,0:T(8,128)S(1)}, u32[]{:S(2)}, u32[]{:S(2)}) %collective-permute-start.12) | collective-permute-done | bytes 49184 | tf_op jit(solution)/shard_map/ppermute | solution.py:207
  94.5 3.2 %collective-permute-start.27 = (bf16[64,768]{1,0:T(8,128)(2,1)S(1)}, bf16[64,768]{1,0:T(8,128)(2,1)S(1)}, u32[]{:S(2)}, u32[]{:S(2)}) collective-permute-start(bf16[64,768]{1,0:T(8,128)(2,1)S(1)} %slice.110), channel_id=1, source_target_pairs={{0,4},{4,0},{8,12},{12,8},{16,20},{20,16},{24,28},{28,24},{32,36},... | collective-permute-start | bytes 294920 | tf_op jit(solution)/shard_map/ppermute | solution.py:38
  102.4 4.6 %collective-permute-done.16.refs_0_ = f32[3,8,512]{2,1,0:T(8,128)S(1)} collective-permute-done((f32[3,8,512]{2,1,0:T(8,128)}, f32[3,8,512]{2,1,0:T(8,128)S(1)}, u32[]{:S(2)}, u32[]{:S(2)}) %collective-permute-start.16) | collective-permute-done | bytes 49184 | tf_op jit(solution)/shard_map/ppermute | solution.py:209
  109.2 3.3 %collective-permute-start.17 = (f32[3,8,512]{2,1,0:T(8,128)}, f32[3,8,512]{2,1,0:T(8,128)S(1)}, u32[]{:S(2)}, u32[]{:S(2)}) collective-permute-start(f32[3,8,512]{2,1,0:T(8,128)} %shard_map.145.own_ref), channel_id=1, source_target_pairs={{0,16},{4,20},{8,24},{12,28},{16,0},{20,4},{24,8},{28,12},{32,48},... | collective-permute-start | bytes 147464 | tf_op jit(solution)/shard_map/ppermute | solution.py:209
  112.6 5.3 %collective-permute-start.28 = (bf16[32,768]{1,0:T(8,128)(2,1)S(1)}, bf16[32,768]{1,0:T(8,128)(2,1)S(1)}, u32[]{:S(2)}, u32[]{:S(2)}) collective-permute-start(bf16[32,768]{1,0:T(8,128)(2,1)S(1)} %slice.112), channel_id=1, source_target_pairs={{0,8},{4,12},{8,0},{12,4},{16,24},{20,28},{24,16},{28,20},{32,40},... | collective-permute-start | bytes 147464 | tf_op jit(solution)/shard_map/ppermute | solution.py:38
  123.4 5.0 %audio_queries.1 = (bf16[768,384]{1,0:T(8,128)(2,1)}, bf16[768,384]{1,0:T(8,128)(2,1)}, f32[128,768]{1,0:T(8,128)S(1)}, bf16[128,768]{1,0:T(8,128)(2,1)S(1)}, bf...) custom-call(f32[3,8,512]{2,1,0:T(8,128)S(1)} %copy-done.4, bf16[768,384]{1,0:T(8,128)(2,1)S(1)} %copy-done, ...), custom_call_target="tpu_custom_call" | custom-call | tf_op jit(solution)/shard_map/audio_queries/pallas_call | solution.py:222
  130.4 4.7 %collective-permute-start.19 = (bf16[128,768]{1,0:T(8,128)(2,1)S(1)}, bf16[128,768]{1,0:T(8,128)(2,1)S(1)}, u32[]{:S(2)}, u32[]{:S(2)}) collective-permute-start(bf16[128,768]{1,0:T(8,128)(2,1)S(1)} %get-tuple-element.23), channel_id=1, source_target_pairs={{0,64},{4,68},{8,72},{12,76},{16,80},{20,84},{24,88},{28,92},{32,9... | collective-permute-start | bytes 589832 | tf_op jit(solution)/shard_map/ppermute | solution.py:35
  139.7 2.9 %collective-permute-done.20 = bf16[128,768]{1,0:T(8,128)(2,1)S(1)} collective-permute-done((bf16[128,768]{1,0:T(8,128)(2,1)S(1)}, bf16[128,768]{1,0:T(8,128)(2,1)S(1)}, u32[]{:S(2)}, u32[]{:S(2)}) %collective-permute-start.20) | collective-permute-done | bytes 196640 | tf_op jit(solution)/shard_map/ppermute | solution.py:35
  149.5 3.3 %collective-permute-start.22 = (bf16[32,768]{1,0:T(8,128)(2,1)S(1)}, bf16[32,768]{1,0:T(8,128)(2,1)S(1)}, u32[]{:S(2)}, u32[]{:S(2)}) collective-permute-start(bf16[32,768]{1,0:T(8,128)(2,1)S(1)} %slice.113), channel_id=1, source_target_pairs={{0,8},{4,12},{8,0},{12,4},{16,24},{20,28},{24,16},{28,20},{32,40},... | collective-permute-start | bytes 147464 | tf_op jit(solution)/shard_map/ppermute | solution.py:38
  153.0 3.4 %collective-permute-done.22 = bf16[32,768]{1,0:T(8,128)(2,1)S(1)} collective-permute-done((bf16[32,768]{1,0:T(8,128)(2,1)S(1)}, bf16[32,768]{1,0:T(8,128)(2,1)S(1)}, u32[]{:S(2)}, u32[]{:S(2)}) %collective-permute-start.22) | collective-permute-done | bytes 49184 | tf_op jit(solution)/shard_map/ppermute | solution.py:38
  156.5 4.4 %collective-permute-start.23 = (bf16[16,768]{1,0:T(8,128)(2,1)S(1)}, bf16[16,768]{1,0:T(8,128)(2,1)S(1)}, u32[]{:S(2)}, u32[]{:S(2)}) collective-permute-start(bf16[16,768]{1,0:T(8,128)(2,1)S(1)} %slice.115), channel_id=1, source_target_pairs={{0,16},{4,20},{8,24},{12,28},{16,0},{20,4},{24,8},{28,12},{32,48},... | collective-permute-start | bytes 73736 | tf_op jit(solution)/shard_map/ppermute | solution.py:38
  161.5 4.6 %collective-permute-done.23 = bf16[16,768]{1,0:T(8,128)(2,1)S(1)} collective-permute-done((bf16[16,768]{1,0:T(8,128)(2,1)S(1)}, bf16[16,768]{1,0:T(8,128)(2,1)S(1)}, u32[]{:S(2)}, u32[]{:S(2)}) %collective-permute-start.23) | collective-permute-done | bytes 24608 | tf_op jit(solution)/shard_map/ppermute | solution.py:38
  (103 shorter events, 58.5 us)
Async XLA Ops:
  1.4 11.1 %collective-permute-start = (bf16[16,768]{1,0:T(8,128)(2,1)S(1)}, bf16[16,768]{1,0:T(8,128)(2,1)S(1)}, u32[]{:S(2)}, u32[]{:S(2)}) collective-permute-start(bf16[16,768]{1,0:T(8,128)(2,1)S(1)} %constant_dynamic-update-slice_fusion), channel_id=1, source_target_pairs={{0,16},{4,20},{8,24},{12,28},{16,0},{20,4},{24,8},{28,12},{32,48},... | collective-permute-start | bytes 73736 | tf_op jit(solution)/shard_map/ppermute | solution.py:28
  10.5 9.8 %collective-permute-start.6 = (bf16[16,768]{1,0:T(8,128)(2,1)S(1)}, bf16[16,768]{1,0:T(8,128)(2,1)S(1)}, u32[]{:S(2)}, u32[]{:S(2)}) collective-permute-start(bf16[16,768]{1,0:T(8,128)(2,1)S(1)} %constant_dynamic-update-slice_fusion.2), channel_id=1, source_target_pairs={{0,16},{4,20},{8,24},{12,28},{16,0},{20,4},{24,8},{28,12},{32,48},... | collective-permute-start | bytes 73736 | tf_op jit(solution)/shard_map/ppermute | solution.py:28
  12.5 13.0 %collective-permute-start.1 = (bf16[32,768]{1,0:T(8,128)(2,1)S(1)}, bf16[32,768]{1,0:T(8,128)(2,1)S(1)}, u32[]{:S(2)}, u32[]{:S(2)}) collective-permute-start(bf16[32,768]{1,0:T(8,128)(2,1)S(1)} %pad_maximum_fusion.4), channel_id=1, source_target_pairs={{0,8},{4,12},{8,0},{12,4},{16,24},{20,28},{24,16},{28,20},{32,40},... | collective-permute-start | bytes 147464 | tf_op jit(solution)/shard_map/ppermute | solution.py:28
  20.4 7.7 %collective-permute-start.7 = (bf16[32,768]{1,0:T(8,128)(2,1)S(1)}, bf16[32,768]{1,0:T(8,128)(2,1)S(1)}, u32[]{:S(2)}, u32[]{:S(2)}) collective-permute-start(bf16[32,768]{1,0:T(8,128)(2,1)S(1)} %pad_maximum_fusion.5), channel_id=1, source_target_pairs={{0,8},{4,12},{8,0},{12,4},{16,24},{20,28},{24,16},{28,20},{32,40},... | collective-permute-start | bytes 147464 | tf_op jit(solution)/shard_map/ppermute | solution.py:28
  28.1 15.7 %collective-permute-start.8 = (bf16[64,768]{1,0:T(8,128)(2,1)S(1)}, bf16[64,768]{1,0:T(8,128)(2,1)S(1)}, u32[]{:S(2)}, u32[]{:S(2)}) collective-permute-start(bf16[64,768]{1,0:T(8,128)(2,1)S(1)} %pad_maximum_fusion.3), channel_id=1, source_target_pairs={{0,4},{4,0},{8,12},{12,8},{16,20},{20,16},{24,28},{28,24},{32,36},... | collective-permute-start | bytes 294920 | tf_op jit(solution)/shard_map/ppermute | solution.py:28
  32.2 17.1 %collective-permute-start.5 = (bf16[128,768]{1,0:T(8,128)(2,1)S(1)}, bf16[128,768]{1,0:T(8,128)(2,1)S(1)}, u32[]{:S(2)}, u32[]{:S(2)}) collective-permute-start(bf16[128,768]{1,0:T(8,128)(2,1)S(1)} %pad_maximum_fusion.refs_0_.refs_4_), channel_id=1, source_target_pairs={{0,32},{4,36},{8,40},{12,44},{16,48},{20,52},{24,56},{28,60},{32,6... | collective-permute-start | bytes 589832 | tf_op jit(solution)/shard_map/ppermute | solution.py:29
  35.7 17.4 %collective-permute-start.4 = (bf16[128,768]{1,0:T(8,128)(2,1)S(1)}, bf16[128,768]{1,0:T(8,128)(2,1)S(1)}, u32[]{:S(2)}, u32[]{:S(2)}) collective-permute-start(bf16[128,768]{1,0:T(8,128)(2,1)S(1)} %pad_maximum_fusion.refs_0_.refs_4_), channel_id=1, source_target_pairs={{0,64},{4,68},{8,72},{12,76},{16,80},{20,84},{24,88},{28,92},{32,9... | collective-permute-start | bytes 589832 | tf_op jit(solution)/shard_map/ppermute | solution.py:29
  40.5 12.6 %collective-permute-start.3 = (bf16[128,768]{1,0:T(8,128)(2,1)S(1)}, bf16[128,768]{1,0:T(8,128)(2,1)S(1)}, u32[]{:S(2)}, u32[]{:S(2)}) collective-permute-start(bf16[128,768]{1,0:T(8,128)(2,1)S(1)} %pad_maximum_fusion.refs_0_.refs_4_), channel_id=1, source_target_pairs={{0,96},{4,100},{8,104},{12,108},{16,112},{20,116},{24,120},{28,124... | collective-permute-start | bytes 589832 | tf_op jit(solution)/shard_map/ppermute | solution.py:29
  43.9 24.5 %collective-permute-start.11 = (bf16[128,768]{1,0:T(8,128)(2,1)S(1)}, bf16[128,768]{1,0:T(8,128)(2,1)S(1)}, u32[]{:S(2)}, u32[]{:S(2)}) collective-permute-start(bf16[128,768]{1,0:T(8,128)(2,1)S(1)} %pad_maximum_fusion.1.refs_0_.refs_4_), channel_id=1, source_target_pairs={{0,32},{4,36},{8,40},{12,44},{16,48},{20,52},{24,56},{28,60},{32,6... | collective-permute-start | bytes 589832 | tf_op jit(solution)/shard_map/ppermute | solution.py:29
  46.6 26.2 %collective-permute-start.10 = (bf16[128,768]{1,0:T(8,128)(2,1)S(1)}, bf16[128,768]{1,0:T(8,128)(2,1)S(1)}, u32[]{:S(2)}, u32[]{:S(2)}) collective-permute-start(bf16[128,768]{1,0:T(8,128)(2,1)S(1)} %pad_maximum_fusion.1.refs_0_.refs_4_), channel_id=1, source_target_pairs={{0,64},{4,68},{8,72},{12,76},{16,80},{20,84},{24,88},{28,92},{32,9... | collective-permute-start | bytes 589832 | tf_op jit(solution)/shard_map/ppermute | solution.py:29
  49.3 23.5 %collective-permute-start.9 = (bf16[128,768]{1,0:T(8,128)(2,1)S(1)}, bf16[128,768]{1,0:T(8,128)(2,1)S(1)}, u32[]{:S(2)}, u32[]{:S(2)}) collective-permute-start(bf16[128,768]{1,0:T(8,128)(2,1)S(1)} %pad_maximum_fusion.1.refs_0_.refs_4_), channel_id=1, source_target_pairs={{0,96},{4,100},{8,104},{12,108},{16,112},{20,116},{24,120},{28,124... | collective-permute-start | bytes 589832 | tf_op jit(solution)/shard_map/ppermute | solution.py:29
  61.6 31.8 %collective-permute-start.24 = (bf16[128,768]{1,0:T(8,128)(2,1)S(1)}, bf16[128,768]{1,0:T(8,128)(2,1)S(1)}, u32[]{:S(2)}, u32[]{:S(2)}) collective-permute-start(bf16[128,768]{1,0:T(8,128)(2,1)S(1)} %get-tuple-element.29), channel_id=1, source_target_pairs={{0,32},{4,36},{8,40},{12,44},{16,48},{20,52},{24,56},{28,60},{32,6... | collective-permute-start | bytes 589832 | tf_op jit(solution)/shard_map/ppermute | solution.py:35
  64.3 29.2 %collective-permute-start.25 = (bf16[128,768]{1,0:T(8,128)(2,1)S(1)}, bf16[128,768]{1,0:T(8,128)(2,1)S(1)}, u32[]{:S(2)}, u32[]{:S(2)}) collective-permute-start(bf16[128,768]{1,0:T(8,128)(2,1)S(1)} %get-tuple-element.30), channel_id=1, source_target_pairs={{0,64},{4,68},{8,72},{12,76},{16,80},{20,84},{24,88},{28,92},{32,9... | collective-permute-start | bytes 589832 | tf_op jit(solution)/shard_map/ppermute | solution.py:35
  68.3 25.2 %collective-permute-start.26 = (bf16[128,768]{1,0:T(8,128)(2,1)S(1)}, bf16[128,768]{1,0:T(8,128)(2,1)}, u32[]{:S(2)}, u32[]{:S(2)}) collective-permute-start(bf16[128,768]{1,0:T(8,128)(2,1)S(1)} %get-tuple-element.31), channel_id=1, source_target_pairs={{0,96},{4,100},{8,104},{12,108},{16,112},{20,116},{24,120},{28,124... | collective-permute-start | bytes 589832 | tf_op jit(solution)/shard_map/ppermute | solution.py:35
  77.5 7.5 %collective-permute-start.13 = (f32[3,8,512]{2,1,0:T(8,128)S(1)}, f32[3,8,512]{2,1,0:T(8,128)S(1)}, u32[]{:S(2)}, u32[]{:S(2)}) collective-permute-start(f32[3,8,512]{2,1,0:T(8,128)S(1)} %audio_stats.1.own_ref), channel_id=1, source_target_pairs={{0,64},{4,68},{8,72},{12,76},{16,80},{20,84},{24,88},{28,92},{32,9... | collective-permute-start | bytes 147464 | tf_op jit(solution)/shard_map/ppermute | solution.py:207
  81.5 7.2 %collective-permute-start.12 = (f32[3,8,512]{2,1,0:T(8,128)S(1)}, f32[3,8,512]{2,1,0:T(8,128)S(1)}, u32[]{:S(2)}, u32[]{:S(2)}) collective-permute-start(f32[3,8,512]{2,1,0:T(8,128)S(1)} %audio_stats.1.own_ref), channel_id=1, source_target_pairs={{0,32},{4,36},{8,40},{12,44},{16,48},{20,52},{24,56},{28,60},{32,6... | collective-permute-start | bytes 147464 | tf_op jit(solution)/shard_map/ppermute | solution.py:207
  94.5 18.0 %collective-permute-start.27 = (bf16[64,768]{1,0:T(8,128)(2,1)S(1)}, bf16[64,768]{1,0:T(8,128)(2,1)S(1)}, u32[]{:S(2)}, u32[]{:S(2)}) collective-permute-start(bf16[64,768]{1,0:T(8,128)(2,1)S(1)} %slice.110), channel_id=1, source_target_pairs={{0,4},{4,0},{8,12},{12,8},{16,20},{20,16},{24,28},{28,24},{32,36},... | collective-permute-start | bytes 294920 | tf_op jit(solution)/shard_map/ppermute | solution.py:38
  109.2 11.3 %collective-permute-start.17 = (f32[3,8,512]{2,1,0:T(8,128)}, f32[3,8,512]{2,1,0:T(8,128)S(1)}, u32[]{:S(2)}, u32[]{:S(2)}) collective-permute-start(f32[3,8,512]{2,1,0:T(8,128)} %shard_map.145.own_ref), channel_id=1, source_target_pairs={{0,16},{4,20},{8,24},{12,28},{16,0},{20,4},{24,8},{28,12},{32,48},... | collective-permute-start | bytes 147464 | tf_op jit(solution)/shard_map/ppermute | solution.py:209
  112.6 24.9 %collective-permute-start.28 = (bf16[32,768]{1,0:T(8,128)(2,1)S(1)}, bf16[32,768]{1,0:T(8,128)(2,1)S(1)}, u32[]{:S(2)}, u32[]{:S(2)}) collective-permute-start(bf16[32,768]{1,0:T(8,128)(2,1)S(1)} %slice.112), channel_id=1, source_target_pairs={{0,8},{4,12},{8,0},{12,4},{16,24},{20,28},{24,16},{28,20},{32,40},... | collective-permute-start | bytes 147464 | tf_op jit(solution)/shard_map/ppermute | solution.py:38
  128.5 11.2 %collective-permute-start.18 = (bf16[128,768]{1,0:T(8,128)(2,1)S(1)}, bf16[128,768]{1,0:T(8,128)(2,1)S(1)}, u32[]{:S(2)}, u32[]{:S(2)}) collective-permute-start(bf16[128,768]{1,0:T(8,128)(2,1)S(1)} %get-tuple-element.22), channel_id=1, source_target_pairs={{0,32},{4,36},{8,40},{12,44},{16,48},{20,52},{24,56},{28,60},{32,6... | collective-permute-start | bytes 589832 | tf_op jit(solution)/shard_map/ppermute | solution.py:35
  130.4 9.3 %collective-permute-start.19 = (bf16[128,768]{1,0:T(8,128)(2,1)S(1)}, bf16[128,768]{1,0:T(8,128)(2,1)S(1)}, u32[]{:S(2)}, u32[]{:S(2)}) collective-permute-start(bf16[128,768]{1,0:T(8,128)(2,1)S(1)} %get-tuple-element.23), channel_id=1, source_target_pairs={{0,64},{4,68},{8,72},{12,76},{16,80},{20,84},{24,88},{28,92},{32,9... | collective-permute-start | bytes 589832 | tf_op jit(solution)/shard_map/ppermute | solution.py:35
  135.1 7.6 %collective-permute-start.20 = (bf16[128,768]{1,0:T(8,128)(2,1)S(1)}, bf16[128,768]{1,0:T(8,128)(2,1)S(1)}, u32[]{:S(2)}, u32[]{:S(2)}) collective-permute-start(bf16[128,768]{1,0:T(8,128)(2,1)S(1)} %get-tuple-element.24), channel_id=1, source_target_pairs={{0,96},{4,100},{8,104},{12,108},{16,112},{20,116},{24,120},{28,124... | collective-permute-start | bytes 589832 | tf_op jit(solution)/shard_map/ppermute | solution.py:35
  137.5 9.6 %collective-permute-start.29 = (bf16[16,768]{1,0:T(8,128)(2,1)S(1)}, bf16[16,768]{1,0:T(8,128)(2,1)S(1)}, u32[]{:S(2)}, u32[]{:S(2)}) collective-permute-start(bf16[16,768]{1,0:T(8,128)(2,1)S(1)} %slice.114), channel_id=1, source_target_pairs={{0,16},{4,20},{8,24},{12,28},{16,0},{20,4},{24,8},{28,12},{32,48},... | collective-permute-start | bytes 73736 | tf_op jit(solution)/shard_map/ppermute | solution.py:38
  156.5 9.6 %collective-permute-start.23 = (bf16[16,768]{1,0:T(8,128)(2,1)S(1)}, bf16[16,768]{1,0:T(8,128)(2,1)S(1)}, u32[]{:S(2)}, u32[]{:S(2)}) collective-permute-start(bf16[16,768]{1,0:T(8,128)(2,1)S(1)} %slice.115), channel_id=1, source_target_pairs={{0,16},{4,20},{8,24},{12,28},{16,0},{20,4},{24,8},{28,12},{32,48},... | collective-permute-start | bytes 73736 | tf_op jit(solution)/shard_map/ppermute | solution.py:38
  (21 other events, 210.3 us)
